TPU v7x, 32 devices: a whole 2x2x4 slice. The times are simulated.
32 devices in a mesh: seq: 8 (over y, x, core), head: 4 (over z).
Axes of the slice: x: 2, y: 2, z: 4, core: 2. Of those that a mesh axis runs over, the one named last changes fastest.
Arguments:
- queries: bfloat16 [16384, 512], P('seq', 'head'), may hold values from -4 to 4
- key_rows: bfloat16 [16384, 512], P('seq', 'head'), may hold values from -4 to 4
- value_rows: bfloat16 [16384, 512], P('seq', 'head'), may hold values from -6 to 6
- norm_gain: float32 [512], P('head'), may hold values from 0.1 to 1.9
- out_grad: bfloat16 [16384, 512], P('seq', 'head'), may hold values from -6 to 6
Outputs:
- normed: bfloat16 [16384, 512], P('seq', 'head')
- query_grad: bfloat16 [16384, 512], P('seq', 'head')
- key_grad: bfloat16 [16384, 512], P('seq', 'head')
- value_grad: bfloat16 [16384, 512], P('seq', 'head')
All inputs are finite; a program needn't handle non-finite values.
Results may differ from a plain program's by a relative error of at most 0.0059.
Values sent between devices are 32-bit elements; how exact they have to be, the bound alone decides.
A program may use at most 64 MiB of HBM per device.

v0:
```python
import jax
import jax.numpy as jnp
from jax import lax
from jax.sharding import PartitionSpec as P

HEAD_DIM = 128
BLOCK = 512


def causal_mask(size):
    row_index = lax.broadcasted_iota(jnp.int32, (size, size), 0)
    col_index = lax.broadcasted_iota(jnp.int32, (size, size), 1)
    return row_index >= col_index


def body(queries, key_rows, value_rows, norm_gain, out_grad):
    tokens_here = queries.shape[0]
    heads_here = queries.shape[1] // HEAD_DIM
    blocks = tokens_here // BLOCK
    block_shape = (blocks, BLOCK, heads_here, HEAD_DIM)
    query4 = queries.reshape(block_shape)
    key4 = key_rows.reshape(block_shape)
    value4 = value_rows.reshape(block_shape)
    width_all = heads_here * HEAD_DIM * lax.axis_size("head")
    mask4 = causal_mask(BLOCK)[None, None]
    position = lax.axis_index("seq")
    states = jnp.einsum("bshd,bshe->bhde", key4, value4, preferred_element_type=jnp.float32)
    totals = jnp.sum(states, 0)
    piece = lax.all_gather(totals[None], "seq", axis=0, tiled=True)
    anchor = jnp.arange(piece.shape[0], dtype=jnp.int32)
    keep = (anchor < position)[:, None, None, None]
    earlier = jnp.sum(jnp.where(keep, piece, 0.0), 0)
    running = jnp.cumsum(states, 0)
    within = jnp.concatenate([jnp.zeros_like(states[:1]), running[:-1]], 0)
    prefix16 = (earlier[None] + within).astype(jnp.bfloat16)
    scores = jnp.einsum("bthd,bshd->bhts", query4, key4, preferred_element_type=jnp.float32)
    attn = jnp.where(mask4, scores, 0.0).astype(jnp.bfloat16)
    output = jnp.einsum("bhts,bshe->bthe", attn, value4, preferred_element_type=jnp.float32)
    output = output + jnp.einsum(
        "bthd,bhde->bthe", query4, prefix16, preferred_element_type=jnp.float32
    )
    gain4 = norm_gain.reshape(heads_here, HEAD_DIM)
    scaled = out_grad.reshape(block_shape).astype(jnp.float32) * gain4
    squares, products = lax.psum(
        (jnp.sum(output * output, (2, 3)), jnp.sum(scaled * output, (2, 3))), "head"
    )
    rstd = lax.rsqrt(squares / width_all + 1e-05)[:, :, None, None]
    normed = (output * rstd * gain4).astype(jnp.bfloat16).reshape(tokens_here, -1)
    mean_prod = (products / width_all)[:, :, None, None]
    dout = (rstd * scaled - output * rstd**3 * mean_prod).astype(jnp.bfloat16)
    grad_states = jnp.einsum("bthd,bthe->bhde", query4, dout, preferred_element_type=jnp.float32)
    grad_total = jnp.sum(grad_states, 0)
    piece = lax.all_gather(grad_total[None], "seq", axis=0, tiled=True)
    anchor = jnp.arange(piece.shape[0], dtype=jnp.int32)
    keep = (anchor > position)[:, None, None, None]
    later = jnp.sum(jnp.where(keep, piece, 0.0), 0)
    behind = jnp.cumsum(grad_states[::-1], 0)[::-1]
    after = jnp.concatenate([behind[1:], jnp.zeros_like(grad_states[:1])], 0)
    suffix16 = (later[None] + after).astype(jnp.bfloat16)
    bmat = jnp.einsum("bthe,bshe->bhts", dout, value4, preferred_element_type=jnp.float32)
    bmat = jnp.where(mask4, bmat, 0.0).astype(jnp.bfloat16)
    query_grad = jnp.einsum("bhts,bshd->bthd", bmat, key4, preferred_element_type=jnp.float32)
    query_grad = query_grad + jnp.einsum(
        "bthe,bhde->bthd", dout, prefix16, preferred_element_type=jnp.float32
    )
    key_grad = jnp.einsum("bhts,bthd->bshd", bmat, query4, preferred_element_type=jnp.float32)
    key_grad = key_grad + jnp.einsum(
        "bshe,bhde->bshd", value4, suffix16, preferred_element_type=jnp.float32
    )
    value_grad = jnp.einsum("bhts,bthe->bshe", attn, dout, preferred_element_type=jnp.float32)
    value_grad = value_grad + jnp.einsum(
        "bshd,bhde->bshe", key4, suffix16, preferred_element_type=jnp.float32
    )
    return (
        normed,
        query_grad.astype(jnp.bfloat16).reshape(tokens_here, -1),
        key_grad.astype(jnp.bfloat16).reshape(tokens_here, -1),
        value_grad.astype(jnp.bfloat16).reshape(tokens_here, -1),
    )


def solution(mesh):
    return jax.shard_map(
        body,
        mesh=mesh,
        in_specs=(
            P("seq", "head"),
            P("seq", "head"),
            P("seq", "head"),
            P("head"),
            P("seq", "head"),
        ),
        out_specs=(P("seq", "head"), P("seq", "head"), P("seq", "head"), P("seq", "head")),
        check_vma=False,
    )
```

profile of v0, /device:TPU:0, one launch (start us, length us, event | category | flops | bytes accessed | tf_op | source)
XLA Modules:
  0.0 71.4 jit_solution(403312878023820120)
XLA Ops:
  0.7 1.0 %copy-done = bf16[2048,128]{1,0:T(8,128)(2,1)S(1)} copy-done((bf16[2048,128]{1,0:T(8,128)(2,1)S(1)}, bf16[2048,128]{1,0:T(8,128)(2,1)}, u32[]{:S(2)}) %copy-start) | copy-done | bytes 524312
  1.8 1.9 %select_convert_fusion.1 = bf16[4,512,512]{2,1,0:T(8,128)(2,1)S(1)} fusion(bf16[4,512,128]{2,1,0:T(8,128)(2,1)S(1)} %bitcast.81, bf16[4,512,128]{2,1,0:T(8,128)(2,1)} %bitcast.89, pred[512,512]{1,0:T(8,128)(4,1)S(1)} %iota_compare_fusion), kind=kOutput, calls=%fused_computation.1 | convolution fusion | flops 270532608 | bytes 3407872 | tf_op jit(solution)/shard_map/bthd,bshd->bhts/dot_general | solution.py:36
  3.7 1.7 %convolution_bitcast_fusion.2 = f32[4,128,512]{1,2,0:T(8,128)} fusion(bf16[4,512,512]{2,1,0:T(8,128)(2,1)S(1)} %select_convert_fusion.1, bf16[4,512,128]{2,1,0:T(8,128)(2,1)S(1)} %bitcast.85), kind=kOutput, calls=%fused_computation.4 | convolution fusion | flops 268435456 | bytes 3670016 | tf_op jit(solution)/shard_map/bhts,bshe->bthe/dot_general | solution.py:38
  5.4 0.3 fusion.26
  5.7 12.4 %all-gather = f32[1024,128]{1,0:T(8,128)} all-gather(f32[128,128]{1,0:T(8,128)S(1)} %get-tuple-element.12), channel_id=2, replica_groups=mesh['seq'=8,'head'=4] {'seq'}, dimensions={0}, use_global_device_ids=true | all-gather | bytes 589824 | tf_op jit(solution)/shard_map/all_gather | solution.py:29
  18.1 1.3 %copy.39 = f32[8,1,128,128]{2,0,3,1:T(8,128)S(1)} copy(f32[8,1,128,128]{3,2,0,1:T(8,128)} %bitcast.93) | data formatting | bytes 1048576 | tf_op jit(solution)/shard_map/all_gather | solution.py:29
  19.4 0.2 select_reduce_fusion
  19.9 2.8 %fusion.9 = (f32[4,512]{1,0:T(4,128)S(1)}, f32[4,512]{1,0:T(4,128)S(1)}, f32[4,512,1,128]{3,1,0,2:T(8,128)}) fusion(bf16[4,512,1,128]{3,1,0,2:T(8,128)(2,1)} %bitcast.95, f32[128]{0:T(128)S(1)} %copy-done.10, f32[4,128,512]{1,2,0:T(8,128)} %convolution_bitcast_fusion.2, bf16[4,512,128]{2,1,0:T(8,128)(2,1)S(1)} %bitcast.82, ...), kind=kOutput, calls=%fused_computation.20 | convolution fusion | flops 69070848 | bytes 3424768 | tf_op jit(solution)/shard_map/bthd,bhde->bthe/dot_general | solution.py:39
  22.7 19.0 %all-reduce.2 = (f32[4,512]{1,0:T(4,128)S(1)}, f32[4,512]{1,0:T(4,128)S(1)}) all-reduce(f32[4,512]{1,0:T(4,128)S(1)} %get-tuple-element.5, f32[4,512]{1,0:T(4,128)S(1)} %get-tuple-element.4), channel_id=1, replica_groups=mesh['seq'=8,'head'=4] {'head'}, use_global_device_ids=true, to_apply=%region_4.5 | all-reduce | flops 4096 | bytes 32768 | tf_op jit(solution)/shard_map/psum | solution.py:44
  41.7 2.8 %fusion.10 = (bf16[4,512,128]{2,1,0:T(8,128)(2,1)S(1)}, bf16[4,512,1,128]{3,1,0,2:T(8,128)(2,1)}) fusion(f32[4,512,1,128]{3,1,0,2:T(8,128)} %get-tuple-element.14, f32[4,512]{1,0:T(4,128)S(1)} %get-tuple-element.17, f32[4,512]{1,0:T(4,128)S(1)} %get-tuple-element.10, f32[128]{0:T(128)S(1)} %copy-done.10, f32[4,512]{1,0:T(4,128)S(1)} %get-tuple-element.11, ...), kind=kLoop, calls=%fused_computation.24 | loop fusion | flops 2621440 | bytes 2646528 | tf_op jit(solution)/shard_map/reshape.36
  44.5 1.5 %fusion.28 = f32[4,128,512]{2,1,0:T(8,128)} fusion(bf16[4,512,128]{2,1,0:T(8,128)(2,1)S(1)} %get-tuple-element.8, bf16[4,512,512]{2,1,0:T(8,128)(2,1)S(1)} %select_convert_fusion.1), kind=kOutput, calls=%fused_computation.47 | convolution fusion | flops 268435456 | bytes 3670016 | tf_op jit(solution)/shard_map/bhts,bthe->bshe/dot_general | solution.py:70
  46.0 1.0 %fusion.27 = (f32[128,128]{0,1:T(8,128)S(1)}, f32[4,128,128]{1,2,0:T(8,128)}) fusion(bf16[4,512,128]{2,1,0:T(8,128)(2,1)S(1)} %get-tuple-element.8, bf16[4,512,128]{2,1,0:T(8,128)(2,1)S(1)} %bitcast.84), kind=kOutput, calls=%fused_computation.46 | convolution fusion | flops 67158016 | bytes 1376256 | tf_op jit(solution)/shard_map/bthd,bthe->bhde/dot_general | solution.py:51
  47.1 11.0 %all-gather.1 = f32[1024,128]{0,1:T(8,128)S(1)} all-gather(f32[128,128]{0,1:T(8,128)S(1)} %get-tuple-element.15), channel_id=3, replica_groups=mesh['seq'=8,'head'=4] {'seq'}, dimensions={0}, use_global_device_ids=true | all-gather | bytes 589824 | tf_op jit(solution)/shard_map/all_gather | solution.py:53
  58.1 0.8 %fusion.11 = f32[128,128]{0,1:T(8,128)} fusion(f32[16,8,8,128]{3,2,1,0:T(8,128)S(1)} %copy.59, pred[8]{0:T(512)(128)(4,1)S(1)} %iota_compare_fusion.1), kind=kLoop, calls=%fused_computation.26 | loop fusion | flops 245760 | bytes 589832 | tf_op jit(solution)/shard_map/reduce_sum | solution.py:56
  59.0 1.0 %reverse.4 = f32[4,128,128]{1,2,0:T(8,128)S(1)} reverse(f32[4,128,128]{1,2,0:T(8,128)} %get-tuple-element.16), dimensions={0} | reverse | bytes 524288 | tf_op jit(solution)/shard_map/reverse
  60.1 0.7 slice.13
  60.8 0.9 %slice.11 = f32[3,1,128,128]{2,3,0,1:T(8,128)S(1)} reverse(f32[3,1,128,128]{2,3,0,1:T(8,128)} %slice.13), dimensions={0} | reverse | bytes 393216 | tf_op jit(solution)/shard_map/slice | solution.py:58
  61.8 1.9 %fusion.4 = bf16[4,512,1,128]{1,3,0,2:T(8,128)(2,1)} fusion(f32[4,128,512]{2,1,0:T(8,128)S(1)} %copy-done.5, bf16[4,512,128]{2,1,0:T(8,128)(2,1)S(1)} %bitcast.91, f32[3,1,128,128]{2,3,0,1:T(8,128)S(1)} %slice.11, f32[128,128]{0,1:T(8,128)} %fusion.11), kind=kOutput, calls=%fused_computation.13 | convolution fusion | flops 67764224 | bytes 2359296 | tf_op jit(solution)/shard_map/bshd,bhde->bshe/dot_general | solution.py:71
  63.7 2.0 %copy.49 = bf16[4,512,1,128]{3,1,0,2:T(8,128)(2,1)} copy(bf16[4,512,1,128]{1,3,0,2:T(8,128)(2,1)} %fusion.4) | data formatting | bytes 1048576 | tf_op jit(solution)/shard_map/convert_element_type | solution.py:78
  65.8 1.7 %select_convert_fusion = bf16[4,512,512]{2,1,0:T(8,128)(2,1)S(1)} fusion(bf16[4,512,128]{2,1,0:T(8,128)(2,1)S(1)} %get-tuple-element.8, bf16[4,512,128]{2,1,0:T(8,128)(2,1)S(1)} %bitcast.87, pred[512,512]{1,0:T(8,128)(4,1)} %copy-done.9), kind=kOutput, calls=%fused_computation | convolution fusion | flops 270532608 | bytes 3407872 | tf_op jit(solution)/shard_map/bthe,bshe->bhts/dot_general | solution.py:60
  67.5 0.9 %convolution_bitcast_fusion = f32[4,128,512]{1,2,0:T(8,128)S(1)} fusion(bf16[4,512,512]{2,1,0:T(8,128)(2,1)S(1)} %select_convert_fusion, bf16[4,512,128]{2,1,0:T(8,128)(2,1)S(1)} %bitcast.83), kind=kOutput, calls=%fused_computation.2 | convolution fusion | flops 268435456 | bytes 3670016 | tf_op jit(solution)/shard_map/bhts,bthd->bshd/dot_general | solution.py:66
  68.4 1.1 %fusion.3 = bf16[4,128,512]{1,2,0:T(8,128)(2,1)} fusion(f32[4,128,512]{1,2,0:T(8,128)S(1)} %convolution_bitcast_fusion, bf16[4,512,128]{2,1,0:T(8,128)(2,1)S(1)} %bitcast.88, f32[3,1,128,128]{2,3,0,1:T(8,128)S(1)} %slice.11, f32[128,128]{0,1:T(8,128)S(1)} %copy-done.8), kind=kOutput, calls=%fused_computation.12 | convolution fusion | flops 67764224 | bytes 2359296 | tf_op jit(solution)/shard_map/bshe,bhde->bshd/dot_general | solution.py:67
  69.5 0.7 convolution_bitcast_fusion.1
  70.3 1.1 %fusion.1 = bf16[4,128,512]{1,2,0:T(8,128)(2,1)} fusion(f32[4,128,512]{1,2,0:T(8,128)S(1)} %convolution_bitcast_fusion.1, bf16[4,512,128]{2,1,0:T(8,128)(2,1)S(1)} %get-tuple-element.8, f32[3,1,128,128]{3,2,0,1:T(8,128)S(1)} %slice.12, f32[128,128]{1,0:T(8,128)S(1)} %copy-done.7), kind=kOutput, calls=%fused_computation.10 | convolution fusion | flops 67764224 | bytes 2359296 | tf_op jit(solution)/shard_map/bthe,bhde->bthd/dot_general | solution.py:63
  (30 shorter events, 0.8 us)
Async XLA Ops:
  0.6 1.0 %copy-start = (bf16[2048,128]{1,0:T(8,128)(2,1)S(1)}, bf16[2048,128]{1,0:T(8,128)(2,1)}, u32[]{:S(2)}) copy-start(bf16[2048,128]{1,0:T(8,128)(2,1)} %param.5) | copy-start | bytes 1572868
  0.6 3.0 %copy-start.1 = (bf16[2048,128]{1,0:T(8,128)(2,1)S(1)}, bf16[2048,128]{1,0:T(8,128)(2,1)}, u32[]{:S(2)}) copy-start(bf16[2048,128]{1,0:T(8,128)(2,1)} %param.7) | copy-start | bytes 1572868
  1.8 3.6 %copy-start.9 = (pred[512,512]{1,0:T(8,128)(4,1)}, pred[512,512]{1,0:T(8,128)(4,1)S(1)}, u32[]{:S(2)}) copy-start(pred[512,512]{1,0:T(8,128)(4,1)S(1)} %iota_compare_fusion) | copy-start | bytes 786436
  3.7 1.7 %copy-start.3 = (bf16[2048,128]{1,0:T(8,128)(2,1)S(1)}, bf16[2048,128]{1,0:T(8,128)(2,1)}, u32[]{:S(2)}) copy-start(bf16[2048,128]{1,0:T(8,128)(2,1)} %param.6) | copy-start | bytes 1572868
  5.4 14.5 %copy-start.10 = (f32[128]{0:T(128)S(1)}, f32[128]{0:T(128)}, u32[]{:S(2)}) copy-start(f32[128]{0:T(128)} %param.8) | copy-start | bytes 1540
  19.7 3.0 %copy-start.6 = (f32[128,128]{1,0:T(8,128)}, f32[128,128]{1,0:T(8,128)S(1)}, u32[]{:S(2)}) copy-start(f32[128,128]{1,0:T(8,128)S(1)} %copy.40) | copy-start | bytes 196612
  47.1 14.7 %copy-start.4 = (bf16[2048,128]{1,0:T(8,128)(2,1)S(1)}, bf16[2048,128]{1,0:T(8,128)(2,1)}, u32[]{:S(2)}) copy-start(bf16[2048,128]{1,0:T(8,128)(2,1)} %param.6) | copy-start | bytes 1572868
  47.1 14.7 %copy-start.5 = (f32[4,128,512]{2,1,0:T(8,128)S(1)}, f32[4,128,512]{2,1,0:T(8,128)}, u32[]{:S(2)}) copy-start(f32[4,128,512]{2,1,0:T(8,128)} %fusion.28) | copy-start | bytes 3145732
  60.1 5.6 %copy-start.2 = (bf16[2048,128]{1,0:T(8,128)(2,1)S(1)}, bf16[2048,128]{1,0:T(8,128)(2,1)}, u32[]{:S(2)}) copy-start(bf16[2048,128]{1,0:T(8,128)(2,1)} %param.7) | copy-start | bytes 1572868
  67.5 0.9 %copy-start.8 = (f32[128,128]{0,1:T(8,128)S(1)}, f32[128,128]{0,1:T(8,128)}, u32[]{:S(2)}) copy-start(f32[128,128]{0,1:T(8,128)} %fusion.11) | copy-start | bytes 196612
  69.5 0.8 %copy-start.7 = (f32[128,128]{1,0:T(8,128)S(1)}, f32[128,128]{1,0:T(8,128)}, u32[]{:S(2)}) copy-start(f32[128,128]{1,0:T(8,128)} %copy-done.6) | copy-start | bytes 196612
where the time goes:
time: 72 us; the launch traced here: 71.4 us
  blocking collectives  42.3 us (59%)
  matrix products  16.7 us (23%)
  local copies, waits for them, and re-layouts  7.31 us (10%)
  other arithmetic  4.29 us (6%)
  between operations  0.84 us (1%)
    psum x1, blocking collectives, body(): lax.psum((jnp.sum(output * output, (2, 3)), jnp.sum(scaled * output, (2,...  19 us
    all_gather x1, blocking collectives, body(): piece = lax.all_gather(totals[None], 'seq', axis=0, tiled=True)  12.4 us
    all_gather x1, blocking collectives, body(): piece = lax.all_gather(grad_total[None], 'seq', axis=0, tiled=True)  11 us
    another operation x1, other arithmetic  2.8 us
    dot_general x1, matrix products, body(): jnp.einsum('bthd,bhde->bthe', query4, prefix16, preferred_element_type=jn...  2.79 us
    convert_element_type x1, local copies, waits for them, and re-layouts, body(): value_grad.astype(jnp.bfloat16).reshape(tokens_here, -1)  2.04 us
    dot_general x1, matrix products, body(): jnp.einsum('bshd,bhde->bshe', key4, suffix16, preferred_element_type=jnp....  1.94 us
    dot_general x1, matrix products, body(): jnp.einsum('bthd,bshd->bhts', query4, key4, preferred_element_type=jnp.fl...  1.88 us

commit v1 on v0

--- a/solution.py
+++ b/solution.py
@@ -50,7 +50,22 @@
     dout = (rstd * scaled - output * rstd**3 * mean_prod).astype(jnp.bfloat16)
     grad_states = jnp.einsum("bthd,bthe->bhde", query4, dout, preferred_element_type=jnp.float32)
     grad_total = jnp.sum(grad_states, 0)
-    piece = lax.all_gather(grad_total[None], "seq", axis=0, tiled=True)
+    field_in = grad_total[None]
+    wide_n = lax.axis_size("seq")
+    series = [field_in]
+    j = 0
+    while j < wide_n - 1:
+        series.append(
+            lax.ppermute(
+                series[-1], axis_name="seq", perm=[(ii, (ii + 1) % wide_n) for ii in range(wide_n)]
+            )
+        )
+        j += 1
+    piece = jnp.roll(
+        jnp.concatenate(series[::-1], axis=0),
+        (lax.axis_index("seq") + 1) * field_in.shape[0],
+        axis=0,
+    )
     anchor = jnp.arange(piece.shape[0], dtype=jnp.int32)
     keep = (anchor > position)[:, None, None, None]
     later = jnp.sum(jnp.where(keep, piece, 0.0), 0)

time: 72 us -> 78.5 us (1.090)
  waiting for transfers between devices: 0 us -> 25.8 us
  blocking collectives: 42.3 us -> 30.3 us
  local copies, waits for them, and re-layouts: 7.31 us -> 1.82 us
  matrix products: 16.7 us -> 15.1 us
    ppermute x0 -> x7, waiting for transfers between devices: none -> 25.8 us  [body(): lax.ppermute(series[-1], axis_name='seq', perm=[(ii, (ii + 1) % wide_n) f...]
    all_gather x1 -> x0, blocking collectives: 11 us -> none  [body(): piece = lax.all_gather(grad_total[None], 'seq', axis=0, tiled=True)]
    dot_general x1, matrix products: 1.94 us -> 0.3 us  [body(): jnp.einsum('bshd,bhde->bshe', key4, suffix16, preferred_element_type=jnp....]
    slice x2, local copies, waits for them, and re-layouts: 1.63 us -> 0.03 us  [body(): after = jnp.concatenate([behind[1:], jnp.zeros_like(grad_states[:1])], 0)]
    dot_general x1, matrix products: 2.79 us -> 1.42 us  [body(): jnp.einsum('bthd,bhde->bthe', query4, prefix16, preferred_element_type=jn...]
    dot_general x1, matrix products: 0.35 us -> 1.6 us  [body(): jnp.einsum('bshd,bshe->bhde', key4, value4, preferred_element_type=jnp.fl...]
    dot_general x1, matrix products: 1.09 us -> 2.3 us  [body(): jnp.einsum('bshe,bhde->bshd', value4, suffix16, preferred_element_type=jn...]
    all_gather x1, local copies, waits for them, and re-layouts: 1.27 us -> 0.19 us  [body(): piece = lax.all_gather(totals[None], 'seq', axis=0, tiled=True)]
  transfers between devices with their start and end apart: 0 -> 7, of which waited for: 0 -> 7; matrix products, arithmetic and copies ran while one was open for 0% -> 8% of each run, Pallas kernels for 0% -> 0%
where the time goes in v1:
time: 78.5 us; the launch traced here: 78.2 us
  blocking collectives  30.3 us (39%)
  waiting for transfers between devices  25.8 us (33%)
  matrix products  15.1 us (19%)
  other arithmetic  4.12 us (5%)
  local copies, waits for them, and re-layouts  1.82 us (2%)
  between operations  0.98 us (1%)
    ppermute x7, waiting for transfers between devices, body(): lax.ppermute(series[-1], axis_name='seq', perm=[(ii, (ii + 1) % wide_n) f...  25.8 us
    psum x1, blocking collectives, body(): lax.psum((jnp.sum(output * output, (2, 3)), jnp.sum(scaled * output, (2,...  19 us
    all_gather x1, blocking collectives, body(): piece = lax.all_gather(totals[None], 'seq', axis=0, tiled=True)  11.3 us
    another operation x1, other arithmetic  2.8 us
    dot_general x1, matrix products, body(): jnp.einsum('bshe,bhde->bshd', value4, suffix16, preferred_element_type=jn...  2.3 us
    dot_general x1, matrix products, body(): jnp.einsum('bhts,bthd->bshd', bmat, query4, preferred_element_type=jnp.fl...  1.9 us
    dot_general x1, matrix products, body(): jnp.einsum('bthd,bshd->bhts', query4, key4, preferred_element_type=jnp.fl...  1.75 us
    dot_general x1, matrix products, body(): jnp.einsum('bshd,bshe->bhde', key4, value4, preferred_element_type=jnp.fl...  1.6 us
  transfers between devices with their start and end apart: 7, of which 7 were waited for; matrix products, arithmetic and copies ran while one was open for 8% of the time, Pallas kernels for 0%

profile of v1, /device:TPU:0, one launch (start us, length us, event | category | flops | bytes accessed | tf_op | source)
XLA Modules:
  0.0 78.2 jit_solution(787992228840418881)
XLA Ops:
  0.6 0.8 iota_compare_fusion
  1.4 1.6 %fusion.25 = (f32[128,128]{1,0:T(8,128)S(1)}, f32[4,128,128]{2,1,0:T(8,128)S(1)}) fusion(bf16[4,512,128]{2,1,0:T(8,128)(2,1)} %bitcast.80, bf16[4,512,128]{2,1,0:T(8,128)(2,1)} %bitcast.84), kind=kOutput, calls=%fused_computation.60 | convolution fusion | flops 67158016 | bytes 1376256 | tf_op jit(solution)/shard_map/bshd,bshe->bhde/dot_general | solution.py:27
  3.2 11.3 %all-gather = f32[1024,128]{1,0:T(8,128)S(1)} all-gather(f32[128,128]{1,0:T(8,128)S(1)} %get-tuple-element.12), channel_id=2, replica_groups=mesh['seq'=8,'head'=4] {'seq'}, dimensions={0}, use_global_device_ids=true | all-gather | bytes 589824 | tf_op jit(solution)/shard_map/all_gather | solution.py:29
  15.0 1.7 %select_convert_fusion.1 = bf16[4,512,512]{2,1,0:T(8,128)(2,1)S(1)} fusion(bf16[4,512,128]{2,1,0:T(8,128)(2,1)S(1)} %bitcast.76, bf16[4,512,128]{2,1,0:T(8,128)(2,1)S(1)} %bitcast.81, pred[512,512]{1,0:T(8,128)(4,1)} %iota_compare_fusion), kind=kOutput, calls=%fused_computation.1 | convolution fusion | flops 270532608 | bytes 3407872 | tf_op jit(solution)/shard_map/bthd,bshd->bhts/dot_general | solution.py:36
  16.8 0.7 convolution_bitcast_fusion.2
  17.5 0.3 copy-done.6
  17.8 1.4 %fusion.9 = (f32[4,512]{1,0:T(4,128)S(1)}, f32[4,512]{1,0:T(4,128)S(1)}, f32[4,512,1,128]{3,1,0,2:T(8,128)}) fusion(bf16[4,512,1,128]{3,1,0,2:T(8,128)(2,1)S(1)} %bitcast.89, f32[128]{0:T(128)S(1)} %copy-done.9, f32[4,128,512]{1,2,0:T(8,128)S(1)} %convolution_bitcast_fusion.2, bf16[4,512,128]{2,1,0:T(8,128)(2,1)S(1)} %bitcast.77, ...), kind=kOutput, calls=%fused_computation.20 | convolution fusion | flops 69070848 | bytes 3424768 | tf_op jit(solution)/shard_map/bthd,bhde->bthe/dot_general | solution.py:39
  19.2 19.0 %all-reduce.2 = (f32[4,512]{1,0:T(4,128)S(1)}, f32[4,512]{1,0:T(4,128)S(1)}) all-reduce(f32[4,512]{1,0:T(4,128)S(1)} %get-tuple-element.5, f32[4,512]{1,0:T(4,128)S(1)} %get-tuple-element.4), channel_id=1, replica_groups=mesh['seq'=8,'head'=4] {'head'}, use_global_device_ids=true, to_apply=%region_4.5 | all-reduce | flops 4096 | bytes 32768 | tf_op jit(solution)/shard_map/psum | solution.py:44
  38.2 2.8 %fusion.10 = (bf16[4,512,128]{2,1,0:T(8,128)(2,1)S(1)}, bf16[4,512,1,128]{3,1,0,2:T(8,128)(2,1)}) fusion(f32[4,512,1,128]{3,1,0,2:T(8,128)} %get-tuple-element.14, f32[4,512]{1,0:T(4,128)S(1)} %get-tuple-element.17, f32[4,512]{1,0:T(4,128)S(1)} %get-tuple-element.10, f32[128]{0:T(128)S(1)} %copy-done.9, f32[4,512]{1,0:T(4,128)S(1)} %get-tuple-element.11, ...), kind=kLoop, calls=%fused_computation.24 | loop fusion | flops 2621440 | bytes 2646528 | tf_op jit(solution)/shard_map/reshape.36
  41.0 1.1 %fusion.26 = (f32[128,128]{0,1:T(8,128)S(1)}, f32[4,128,128]{1,2,0:T(8,128)}) fusion(bf16[4,512,128]{2,1,0:T(8,128)(2,1)S(1)} %get-tuple-element.8, bf16[4,512,128]{2,1,0:T(8,128)(2,1)S(1)} %bitcast.79), kind=kOutput, calls=%fused_computation.61 | convolution fusion | flops 67158016 | bytes 1376256 | tf_op jit(solution)/shard_map/bthd,bthe->bhde/dot_general | solution.py:51
  42.1 1.5 %fusion.27 = f32[4,128,512]{2,1,0:T(8,128)} fusion(bf16[4,512,128]{2,1,0:T(8,128)(2,1)S(1)} %get-tuple-element.8, bf16[4,512,512]{2,1,0:T(8,128)(2,1)S(1)} %select_convert_fusion.1), kind=kOutput, calls=%fused_computation.62 | convolution fusion | flops 268435456 | bytes 3670016 | tf_op jit(solution)/shard_map/bhts,bthe->bshe/dot_general | solution.py:85
  43.7 3.1 %collective-permute-done = f32[1,1,128,128]{2,3,1,0:T(8,128)S(1)} collective-permute-done((f32[1,1,128,128]{2,3,1,0:T(8,128)S(1)}, f32[1,1,128,128]{2,3,1,0:T(8,128)S(1)}, u32[]{:S(2)}, u32[]{:S(2)}) %collective-permute-start) | collective-permute-done | bytes 65568 | tf_op jit(solution)/shard_map/ppermute | solution.py:59
  46.7 0.8 select_convert_fusion
  47.5 3.8 %collective-permute-done.1 = f32[1,1,128,128]{2,3,1,0:T(8,128)S(1)} collective-permute-done((f32[1,1,128,128]{2,3,1,0:T(8,128)S(1)}, f32[1,1,128,128]{2,3,1,0:T(8,128)S(1)}, u32[]{:S(2)}, u32[]{:S(2)}) %collective-permute-start.1) | collective-permute-done | bytes 65568 | tf_op jit(solution)/shard_map/ppermute | solution.py:59
  51.3 1.9 %convolution_bitcast_fusion = f32[4,128,512]{1,2,0:T(8,128)} fusion(bf16[4,512,512]{2,1,0:T(8,128)(2,1)S(1)} %select_convert_fusion, bf16[4,512,128]{2,1,0:T(8,128)(2,1)S(1)} %bitcast.78), kind=kOutput, calls=%fused_computation.2 | convolution fusion | flops 268435456 | bytes 3670016 | tf_op jit(solution)/shard_map/bhts,bthd->bshd/dot_general | solution.py:81
  53.2 2.7 %collective-permute-done.2 = f32[1,1,128,128]{2,3,1,0:T(8,128)S(1)} collective-permute-done((f32[1,1,128,128]{2,3,1,0:T(8,128)S(1)}, f32[1,1,128,128]{2,3,1,0:T(8,128)S(1)}, u32[]{:S(2)}, u32[]{:S(2)}) %collective-permute-start.2) | collective-permute-done | bytes 65568 | tf_op jit(solution)/shard_map/ppermute | solution.py:59
  55.9 0.7 convolution_bitcast_fusion.1
  56.6 3.9 %collective-permute-done.3 = f32[1,1,128,128]{2,3,1,0:T(8,128)S(1)} collective-permute-done((f32[1,1,128,128]{2,3,1,0:T(8,128)S(1)}, f32[1,1,128,128]{2,3,1,0:T(8,128)S(1)}, u32[]{:S(2)}, u32[]{:S(2)}) %collective-permute-start.3) | collective-permute-done | bytes 65568 | tf_op jit(solution)/shard_map/ppermute | solution.py:59
  60.5 1.1 %fusion.1 = bf16[4,128,512]{1,2,0:T(8,128)(2,1)} fusion(f32[4,128,512]{1,2,0:T(8,128)S(1)} %convolution_bitcast_fusion.1, bf16[4,512,128]{2,1,0:T(8,128)(2,1)S(1)} %get-tuple-element.8, f32[3,1,128,128]{3,2,0,1:T(8,128)S(1)} %slice.12, f32[128,128]{1,0:T(8,128)S(1)} %copy.51), kind=kOutput, calls=%fused_computation.10 | convolution fusion | flops 67764224 | bytes 2359296 | tf_op jit(solution)/shard_map/bthe,bhde->bthd/dot_general | solution.py:78
  61.6 3.5 %collective-permute-done.4 = f32[1,1,128,128]{2,3,1,0:T(8,128)S(1)} collective-permute-done((f32[1,1,128,128]{2,3,1,0:T(8,128)S(1)}, f32[1,1,128,128]{2,3,1,0:T(8,128)S(1)}, u32[]{:S(2)}, u32[]{:S(2)}) %collective-permute-start.4) | collective-permute-done | bytes 65568 | tf_op jit(solution)/shard_map/ppermute | solution.py:59
  65.3 4.4 %collective-permute-done.5 = f32[1,1,128,128]{2,3,1,0:T(8,128)S(1)} collective-permute-done((f32[1,1,128,128]{2,3,1,0:T(8,128)S(1)}, f32[1,1,128,128]{2,3,1,0:T(8,128)S(1)}, u32[]{:S(2)}, u32[]{:S(2)}) %collective-permute-start.5) | collective-permute-done | bytes 65568 | tf_op jit(solution)/shard_map/ppermute | solution.py:59
  69.7 4.6 %collective-permute-done.6 = f32[1,1,128,128]{2,3,1,0:T(8,128)S(1)} collective-permute-done((f32[1,1,128,128]{2,3,1,0:T(8,128)S(1)}, f32[1,1,128,128]{2,3,1,0:T(8,128)S(1)}, u32[]{:S(2)}, u32[]{:S(2)}) %collective-permute-start.6) | collective-permute-done | bytes 65568 | tf_op jit(solution)/shard_map/ppermute | solution.py:59
  74.9 1.0 %copy.60 = bf16[4,512,1,128]{3,1,0,2:T(8,128)(2,1)} copy(bf16[4,512,1,128]{1,3,0,2:T(8,128)(2,1)S(1)} %fusion.4) | data formatting | bytes 1048576 | tf_op jit(solution)/shard_map/convert_element_type | solution.py:93
  75.9 2.3 %fusion.3 = bf16[4,128,512]{1,2,0:T(8,128)(2,1)} fusion(f32[4,128,512]{1,2,0:T(8,128)} %convolution_bitcast_fusion, bf16[4,512,128]{2,1,0:T(8,128)(2,1)S(1)} %bitcast.87, f32[3,1,128,128]{2,3,0,1:T(8,128)S(1)} %slice.11, f32[128,128]{0,1:T(8,128)S(1)} %select_reduce_fusion), kind=kOutput, calls=%fused_computation.12 | convolution fusion | flops 67764224 | bytes 2359296 | tf_op jit(solution)/shard_map/bshe,bhde->bshd/dot_general | solution.py:82
  (56 shorter events, 1.4 us)
Async XLA Ops:
  0.6 14.3 %copy-start = (bf16[2048,128]{1,0:T(8,128)(2,1)S(1)}, bf16[2048,128]{1,0:T(8,128)(2,1)}, u32[]{:S(2)}) copy-start(bf16[2048,128]{1,0:T(8,128)(2,1)} %param.5) | copy-start | bytes 1572868
  1.4 13.5 %copy-start.1 = (bf16[2048,128]{1,0:T(8,128)(2,1)S(1)}, bf16[2048,128]{1,0:T(8,128)(2,1)}, u32[]{:S(2)}) copy-start(bf16[2048,128]{1,0:T(8,128)(2,1)} %param.6) | copy-start | bytes 1572868
  15.0 1.8 %copy-start.2 = (bf16[2048,128]{1,0:T(8,128)(2,1)S(1)}, bf16[2048,128]{1,0:T(8,128)(2,1)}, u32[]{:S(2)}) copy-start(bf16[2048,128]{1,0:T(8,128)(2,1)} %param.7) | copy-start | bytes 1572868
  16.8 1.0 %copy-start.6 = (bf16[2048,128]{1,0:T(8,128)(2,1)S(1)}, bf16[2048,128]{1,0:T(8,128)(2,1)}, u32[]{:S(2)}) copy-start(bf16[2048,128]{1,0:T(8,128)(2,1)} %param.9) | copy-start | bytes 1572868
  16.8 1.0 %copy-start.9 = (f32[128]{0:T(128)S(1)}, f32[128]{0:T(128)}, u32[]{:S(2)}) copy-start(f32[128]{0:T(128)} %param.8) | copy-start | bytes 1540
  42.1 4.6 %copy-start.3 = (bf16[2048,128]{1,0:T(8,128)(2,1)S(1)}, bf16[2048,128]{1,0:T(8,128)(2,1)}, u32[]{:S(2)}) copy-start(bf16[2048,128]{1,0:T(8,128)(2,1)} %param.7) | copy-start | bytes 1572868
  42.1 4.6 %copy-start.8 = (pred[512,512]{1,0:T(8,128)(4,1)S(1)}, pred[512,512]{1,0:T(8,128)(4,1)}, u32[]{:S(2)}) copy-start(pred[512,512]{1,0:T(8,128)(4,1)} %iota_compare_fusion) | copy-start | bytes 786436
  42.1 4.6 %collective-permute-start = (f32[1,1,128,128]{2,3,1,0:T(8,128)S(1)}, f32[1,1,128,128]{2,3,1,0:T(8,128)S(1)}, u32[]{:S(2)}, u32[]{:S(2)}) collective-permute-start(f32[1,1,128,128]{2,3,1,0:T(8,128)S(1)} %bitcast.90), channel_id=1, source_target_pairs={{0,4},{4,8},{8,12},{12,16},{16,20},{20,24},{24,28},{28,0},{1,5},{5... | collective-permute-start | bytes 196616 | tf_op jit(solution)/shard_map/ppermute | solution.py:59
  46.7 4.6 %collective-permute-start.1 = (f32[1,1,128,128]{2,3,1,0:T(8,128)S(1)}, f32[1,1,128,128]{2,3,1,0:T(8,128)S(1)}, u32[]{:S(2)}, u32[]{:S(2)}) collective-permute-start(f32[1,1,128,128]{2,3,1,0:T(8,128)S(1)} %collective-permute-done), channel_id=1, source_target_pairs={{0,4},{4,8},{8,12},{12,16},{16,20},{20,24},{24,28},{28,0},{1,5},{5... | collective-permute-start | bytes 196616 | tf_op jit(solution)/shard_map/ppermute | solution.py:59
  51.3 4.6 %collective-permute-start.2 = (f32[1,1,128,128]{2,3,1,0:T(8,128)S(1)}, f32[1,1,128,128]{2,3,1,0:T(8,128)S(1)}, u32[]{:S(2)}, u32[]{:S(2)}) collective-permute-start(f32[1,1,128,128]{2,3,1,0:T(8,128)S(1)} %collective-permute-done.1), channel_id=1, source_target_pairs={{0,4},{4,8},{8,12},{12,16},{16,20},{20,24},{24,28},{28,0},{1,5},{5... | collective-permute-start | bytes 196616 | tf_op jit(solution)/shard_map/ppermute | solution.py:59
  55.9 4.6 %collective-permute-start.3 = (f32[1,1,128,128]{2,3,1,0:T(8,128)S(1)}, f32[1,1,128,128]{2,3,1,0:T(8,128)S(1)}, u32[]{:S(2)}, u32[]{:S(2)}) collective-permute-start(f32[1,1,128,128]{2,3,1,0:T(8,128)S(1)} %collective-permute-done.2), channel_id=1, source_target_pairs={{0,4},{4,8},{8,12},{12,16},{16,20},{20,24},{24,28},{28,0},{1,5},{5... | collective-permute-start | bytes 196616 | tf_op jit(solution)/shard_map/ppermute | solution.py:59
  56.6 5.0 %copy-start.7 = (f32[4,128,128]{1,2,0:T(8,128)S(1)}, f32[4,128,128]{1,2,0:T(8,128)}, u32[]{:S(2)}) copy-start(f32[4,128,128]{1,2,0:T(8,128)} %get-tuple-element.16) | copy-start | bytes 786436
  60.5 4.6 %collective-permute-start.4 = (f32[1,1,128,128]{2,3,1,0:T(8,128)S(1)}, f32[1,1,128,128]{2,3,1,0:T(8,128)S(1)}, u32[]{:S(2)}, u32[]{:S(2)}) collective-permute-start(f32[1,1,128,128]{2,3,1,0:T(8,128)S(1)} %collective-permute-done.3), channel_id=1, source_target_pairs={{0,4},{4,8},{8,12},{12,16},{16,20},{20,24},{24,28},{28,0},{1,5},{5... | collective-permute-start | bytes 196616 | tf_op jit(solution)/shard_map/ppermute | solution.py:59
  61.6 13.0 %copy-start.5 = (f32[4,128,512]{2,1,0:T(8,128)S(1)}, f32[4,128,512]{2,1,0:T(8,128)}, u32[]{:S(2)}) copy-start(f32[4,128,512]{2,1,0:T(8,128)} %fusion.27) | copy-start | bytes 3145732
  65.1 4.6 %collective-permute-start.5 = (f32[1,1,128,128]{2,3,1,0:T(8,128)S(1)}, f32[1,1,128,128]{2,3,1,0:T(8,128)S(1)}, u32[]{:S(2)}, u32[]{:S(2)}) collective-permute-start(f32[1,1,128,128]{2,3,1,0:T(8,128)S(1)} %collective-permute-done.4), channel_id=1, source_target_pairs={{0,4},{4,8},{8,12},{12,16},{16,20},{20,24},{24,28},{28,0},{1,5},{5... | collective-permute-start | bytes 196616 | tf_op jit(solution)/shard_map/ppermute | solution.py:59
  69.7 4.6 %collective-permute-start.6 = (f32[1,1,128,128]{2,3,1,0:T(8,128)S(1)}, f32[1,1,128,128]{2,3,1,0:T(8,128)S(1)}, u32[]{:S(2)}, u32[]{:S(2)}) collective-permute-start(f32[1,1,128,128]{2,3,1,0:T(8,128)S(1)} %collective-permute-done.5), channel_id=1, source_target_pairs={{0,4},{4,8},{8,12},{12,16},{16,20},{20,24},{24,28},{28,0},{1,5},{5... | collective-permute-start | bytes 196616 | tf_op jit(solution)/shard_map/ppermute | solution.py:59
  74.5 1.5 %copy-start.4 = (bf16[2048,128]{1,0:T(8,128)(2,1)S(1)}, bf16[2048,128]{1,0:T(8,128)(2,1)}, u32[]{:S(2)}) copy-start(bf16[2048,128]{1,0:T(8,128)(2,1)} %param.7) | copy-start | bytes 1572868
